TPU v7x, 512 devices: a whole 4x4x16 slice. The times are simulated.
512 devices in a mesh: ctx: 64 (over y, z), ch: 8 (over x, core).
Axes of the slice: x: 4, y: 4, z: 16, core: 2. Of those that a mesh axis runs over, the one named last changes fastest.
Arguments:
- query_rows: bfloat16 [8192, 8192], P('ctx', 'ch'), may hold values from -6 to 6
- key_rows: bfloat16 [8192, 8192], P('ctx', 'ch'), may hold values from -6 to 6
- value_rows: bfloat16 [8192, 8192], P('ctx', 'ch'), may hold values from -6 to 6
- short_filter: float32 [3, 3, 8192], P(None, None, 'ch'), may hold values from -3.5 to 3.5
- decay_rate: float32 [8192, 16], P('ch'), may hold values from 2e-05 to 0.1
- residues: float32 [8192, 16], P('ch'), may hold values from -1.5 to 1.5
- out_weight: bfloat16 [8192, 4096], P('ctx', 'ch'), may hold values from -0.1875 to 0.1875
- record_starts: int32 [4], replicated, may hold values from 0 to 8191, as said below
Outputs:
- block_out: bfloat16 [8192, 4096], P('ctx', 'ch')
Inputs may be any that keep to these rules, and one draw needn't show every extreme that they name: record_starts[0] is 0 and the last entry is 8191; the entries are distinct and increasing, and all but the first lie in the second half of the 8192 tokens.
All inputs are finite; a program needn't handle non-finite values.
Results may differ from a plain program's by a relative error of at most 0.017.
Values may be sent and summed in bfloat16 or wider, within the bound.
A program may use at most 64 MiB of HBM per device.

v0:
```python
import jax
import jax.numpy as jnp
from jax import lax
from jax.sharding import PartitionSpec as P

MODES = 16
KS = 3


def shifted(block, axis, distance):
    devices = range(lax.axis_size(axis))
    route = [(i - distance, i) for i in devices if i - distance in devices]
    return lax.ppermute(block, axis, route)


def carried_in(x, axis, combine, identity):
    devices, mine = (lax.axis_size(axis), lax.axis_index(axis))
    everything = jax.tree.map(lambda part: lax.all_gather(part, axis), x)
    start = jax.tree.map(
        lambda part, zero: jnp.broadcast_to(jnp.asarray(zero, part.dtype), part.shape), x, identity
    )

    def hop(k, before):
        reached = k < mine
        new = combine(before, jax.tree.map(lambda part: part[k], everything))
        return jax.tree.map(lambda a, b: jnp.where(reached, a, b), new, before)

    return lax.fori_loop(0, devices, hop, start)


def ages_of(positions, record_starts):
    earlier = record_starts[None, :] <= positions[:, None]
    segment = jnp.max(jnp.where(earlier, record_starts[None, :], 0), axis=1)
    return positions - segment


def masked_conv(extended, weights, ages, count):
    taps = weights.shape[0]
    total = jnp.zeros((count, extended.shape[1]), jnp.float32)
    for tap_index in range(taps):
        keeper = (ages >= tap_index).astype(jnp.float32)[:, None]
        window = extended[taps - 1 - tap_index : taps - 1 - tap_index + count]
        total = total + weights[tap_index][None, :] * window * keeper
    return total


def combine_pairs(earlier, later_pair):
    return (earlier[0] * later_pair[0], later_pair[0] * earlier[1] + later_pair[1])


def local(
    query_rows, key_rows, value_rows, short_filter, decay_rate, residues, out_weight, record_starts
):
    row_count, channels = query_rows.shape
    anchor = lax.axis_index("ctx") * row_count
    positions = anchor + jnp.arange(row_count, dtype=jnp.int32)
    ages = ages_of(positions, record_starts)
    reach_short = KS - 1
    tails = shifted(
        (
            query_rows[row_count - reach_short :],
            key_rows[row_count - reach_short :],
            value_rows[row_count - reach_short :],
        ),
        "ctx",
        1,
    )
    query_conv = masked_conv(
        jnp.concatenate([tails[0], query_rows], axis=0).astype(jnp.float32),
        short_filter[0],
        ages,
        row_count,
    )
    key_conv = masked_conv(
        jnp.concatenate([tails[1], key_rows], axis=0).astype(jnp.float32),
        short_filter[1],
        ages,
        row_count,
    )
    value_conv = masked_conv(
        jnp.concatenate([tails[2], value_rows], axis=0).astype(jnp.float32),
        short_filter[2],
        ages,
        row_count,
    )
    mixed = (key_conv * value_conv).astype(jnp.bfloat16).astype(jnp.float32)
    gain = jnp.sqrt(1.0 - jnp.exp(-2.0 * decay_rate))
    block_rows = 8
    block_count = row_count // block_rows
    inner_index = jnp.arange(block_rows, dtype=jnp.float32)
    inner_ints = jnp.arange(block_rows, dtype=jnp.int32)
    rising = jnp.exp(-decay_rate[None, :, :] * inner_index[:, None, None])
    taps_inner = jnp.sum(rising * (residues * gain)[None, :, :], axis=2)
    local_index = jnp.arange(row_count, dtype=jnp.int32)
    inner_ages = jnp.minimum(ages, local_index % block_rows)
    padded_mixed = jnp.concatenate(
        [jnp.zeros((block_rows - 1, channels), jnp.float32), mixed], axis=0
    )
    within = masked_conv(padded_mixed, taps_inner, inner_ages, row_count)
    entry_powers = jnp.exp(-decay_rate[None, :, :] * (inner_index[:, None, None] + 1.0))
    final_powers = (
        jnp.exp(-decay_rate[None, :, :] * (block_rows - 1.0 - inner_index[:, None, None]))
        * gain[None, :, :]
    )
    block_decay = jnp.exp(-decay_rate * block_rows)
    mixed_blocks = mixed.reshape(block_count, block_rows, channels)
    age_blocks = ages.reshape(block_count, block_rows)
    last_ages = age_blocks[:, block_rows - 1]
    weighted = (last_ages[:, None] >= block_rows - 1 - inner_ints[None, :]).astype(jnp.float32)
    endings = jnp.einsum("rcm,brc->bcm", final_powers, mixed_blocks * weighted[:, :, None])
    unbroken = (last_ages >= block_rows).astype(jnp.float32)

    def advance(state, inputs):
        ending, kept = inputs
        return (block_decay * kept * state + ending, state)

    local_state, entering_states = lax.scan(
        advance, jnp.zeros((channels, MODES), jnp.float32), (endings, unbroken)
    )
    entering = (age_blocks > inner_ints[None, :]).astype(jnp.float32)
    between = (
        jnp.einsum("rcm,bcm->brc", entry_powers, residues[None, :, :] * entering_states)
        * entering[:, :, None]
    )
    device_decay = jnp.exp(-decay_rate * row_count) * (ages[row_count - 1] >= row_count).astype(
        jnp.float32
    )
    identity_pair = (jnp.ones_like(device_decay), jnp.zeros_like(local_state))
    carried = carried_in((device_decay, local_state), "ctx", combine_pairs, identity_pair)[1]
    block_index = jnp.arange(block_count, dtype=jnp.float32)
    block_starts = jnp.exp(-decay_rate[None, :, :] * (block_index[:, None, None] * block_rows))
    coefficient = block_starts * (residues * carried)[None, :, :]
    correction = jnp.einsum("rcm,bcm->brc", entry_powers, coefficient).reshape(row_count, channels)
    untouched = (ages > local_index).astype(jnp.float32)[:, None]
    filtered = within + between.reshape(row_count, channels) + correction * untouched
    gated = (query_conv * filtered).astype(jnp.bfloat16)
    all_channels = lax.all_gather(gated, "ch", axis=1, tiled=True)
    result = jnp.dot(
        all_channels,
        lax.all_gather(out_weight, "ctx", axis=0, tiled=True),
        preferred_element_type=jnp.float32,
    )
    return result.astype(jnp.bfloat16)


def solution(mesh):
    return jax.shard_map(
        local,
        mesh=mesh,
        in_specs=(
            P("ctx", "ch"),
            P("ctx", "ch"),
            P("ctx", "ch"),
            P(None, None, "ch"),
            P("ch", None),
            P("ch", None),
            P("ctx", "ch"),
            P(),
        ),
        out_specs=P("ctx", "ch"),
        check_vma=False,
    )
```

profile of v0, /device:TPU:32, one launch (start us, length us, event | category | flops | bytes accessed | tf_op | source)
XLA Modules:
  0.0 616.6 jit_solution(5873278730106274515)
XLA Ops:
  7.3 3.8 collective-permute-start.1
  11.8 3.8 collective-permute-start.2
  17.6 1.6 fusion.59
  23.6 2.8 copy.59
  26.3 5.7 fusion.16
  32.1 5.2 copy.61
  37.3 32.3 %while.27 = (s32[]{:T(128)}, f32[1024,16]{0,1:T(8,128)S(1)}, f32[16,1024,16]{1,2,0:T(8,128)}, f32[16]{0:T(128)S(1)}, f32[1024,16]{0,1:T(8,128)S(1)}, /*index=5*/f32[16,1024,16]{1,2,0:T(8,128)S(1)}, s32[]{:T(128)}, s32[]{:T(128)}) while((s32[]{:T(128)}, f32[1024,16]{0,1:T(8,128)S(1)}, f32[16,1024,16]{1,2,0:T(8,128)}, ...), condition=%wide.region_3.4_spmd.clone, body=%wide.region_2.3_spmd.clone.sunk | while | flops 81923 | bytes 393844 | solution.py:117
  70.3 5.0 collective-permute-start
  76.8 2.1 slice_reduce_fusion.7
  79.1 4.9 copy.62
  84.0 6.5 %multiply_bitcast_fusion = f32[16,8,1024]{0,1,2:T(8,128)} fusion(bf16[16,1024,16]{2,0,1:T(8,128)(2,1)} %copy.62, f32[16,8]{0,1:T(8,128)S(1)} %copy.63, f32[8]{0:T(128)S(1)} %iota_add_fusion, f32[1024,16]{1,0:T(8,128)S(1)} %copy.57), kind=kOutput, calls=%fused_computation.16 | convolution fusion | flops 4456448 | bytes 1114656 | tf_op jit(solution)/shard_map/rcm,bcm->brc/dot_general | solution.py:122
  90.5 3.0 copy.64
  93.6 74.4 %all-gather.11.cloned.1.call-done = f32[65536,16]{0,1:T(8,128)} async-done(((f32[1024,16]{0,1:T(8,128)}), f32[65536,16]{0,1:T(8,128)}) %all-gather.11.cloned.1.call-update) | async-done | bytes 4194320 | tf_op jit(solution)/shard_map/all_gather | solution.py:18
  168.0 6.5 %copy.72 = f32[2,8,64,1024]{3,2,1,0:T(8,128)} copy(f32[2,8,64,1024]{3,1,2,0:T(8,128)} %bitcast.68) | data formatting | bytes 8388608
  174.5 137.7 %all-gather.13.cloned.1.call-done = f32[65536,16]{0,1:T(8,128)} async-done(((f32[1024,16]{0,1:T(8,128)}), f32[65536,16]{0,1:T(8,128)}) %all-gather.13.cloned.1.call-update) | async-done | bytes 4194320 | tf_op jit(solution)/shard_map/all_gather | solution.py:18
  312.3 6.6 %copy.73 = f32[2,8,64,1024]{3,2,1,0:T(8,128)} copy(f32[2,8,64,1024]{3,1,2,0:T(8,128)} %bitcast.69) | data formatting | bytes 8388608
  318.9 88.1 %while.28 = (s32[]{:T(128)}, f32[1024,16]{0,1:T(8,128)S(1)}, s32[]{:T(128)}, f32[64,1024,16]{1,0,2:T(8,128)}, f32[64,1024,16]{1,0,2:T(8,128)}, /*index=5*/s32[]{:T(128)}, s32[]{:T(128)}) while((s32[]{:T(128)}, f32[1024,16]{0,1:T(8,128)S(1)}, s32[]{:T(128)}, f32[64,1024,16]{1,0,2:T(8,128)}, f32[64,1024,16]{1,0,2:T(8,128)}, ...), condition=%wide.region_5.6_spmd.clone, body=%wide.region_4.5_spmd.clone.sunk | while | flops 65540 | bytes 524389 | solution.py:28
  320.2 1.3 constant_dynamic-slice_fusion.3
  321.6 1.3 constant_dynamic-slice_fusion.3
  323.0 1.3 constant_dynamic-slice_fusion.3
  324.4 1.3 constant_dynamic-slice_fusion.3
  325.7 1.3 constant_dynamic-slice_fusion.3
  327.1 1.3 constant_dynamic-slice_fusion.3
  328.5 1.3 constant_dynamic-slice_fusion.3
  329.9 1.3 constant_dynamic-slice_fusion.3
  331.2 1.3 constant_dynamic-slice_fusion.3
  332.6 1.3 constant_dynamic-slice_fusion.3
  334.0 1.3 constant_dynamic-slice_fusion.3
  335.4 1.3 constant_dynamic-slice_fusion.3
  338.1 1.3 constant_dynamic-slice_fusion.3
  339.5 1.3 constant_dynamic-slice_fusion.3
  340.9 1.3 constant_dynamic-slice_fusion.3
  342.3 1.3 constant_dynamic-slice_fusion.3
  345.0 1.3 constant_dynamic-slice_fusion.3
  346.4 1.3 constant_dynamic-slice_fusion.3
  347.8 1.3 constant_dynamic-slice_fusion.3
  349.1 1.3 constant_dynamic-slice_fusion.3
  350.5 1.3 constant_dynamic-slice_fusion.3
  351.9 1.3 constant_dynamic-slice_fusion.3
  353.3 1.3 constant_dynamic-slice_fusion.3
  354.6 1.3 constant_dynamic-slice_fusion.3
  356.0 1.3 constant_dynamic-slice_fusion.3
  407.2 3.9 fusion.21
  411.0 3.0 copy.69
  414.0 1.7 fusion.47
  416.3 27.3 %all-gather.7.cloned.1.call-done = bf16[128,8192]{1,0:T(8,128)(2,1)} async-done(((bf16[128,1024]{1,0:T(8,128)(2,1)}), bf16[128,8192]{1,0:T(8,128)(2,1)}) %all-gather.7.cloned.1.call-update) | async-done | bytes 2097168 | tf_op jit(solution)/shard_map/all_gather | solution.py:137
  443.7 160.5 %all-gather.9.cloned.1.call-done = bf16[8192,512]{1,0:T(8,128)(2,1)} async-done(((bf16[128,512]{1,0:T(8,128)(2,1)}), bf16[8192,512]{1,0:T(8,128)(2,1)}) %all-gather.9.cloned.1.call-update) | async-done | bytes 8388624 | tf_op jit(solution)/shard_map/all_gather | solution.py:140
  604.1 5.9 convolution_convert_fusion
  (203 shorter events, 95.7 us)
Async XLA Ops:
  6.5 161.5 %all-gather.11.cloned.1.call-start = ((), (), s32[]{:S(2)}) async-start(), calls=%async_computation.2 | async-start | bytes 4259840 | tf_op jit(solution)/shard_map/all_gather | solution.py:18
  7.3 13.7 %collective-permute-start.1 = (bf16[2,1024]{1,0:T(2,128)(2,1)S(1)}, bf16[2,1024]{1,0:T(2,128)(2,1)S(1)}, u32[]{:S(2)}, u32[]{:S(2)}) collective-permute-start(bf16[2,1024]{1,0:T(2,128)(2,1)S(1)} %slice.146), channel_id=1, source_target_pairs={{0,8},{8,16},{16,24},{24,32},{32,40},{40,48},{48,56},{56,64},{64,7... | collective-permute-start | bytes 12296 | tf_op jit(solution)/shard_map/ppermute | solution.py:13
  11.8 10.2 %collective-permute-start.2 = (bf16[2,1024]{1,0:T(2,128)(2,1)S(1)}, bf16[2,1024]{1,0:T(2,128)(2,1)S(1)}, u32[]{:S(2)}, u32[]{:S(2)}) collective-permute-start(bf16[2,1024]{1,0:T(2,128)(2,1)S(1)} %slice.153), channel_id=1, source_target_pairs={{0,8},{8,16},{16,24},{24,32},{32,40},{40,48},{48,56},{56,64},{64,7... | collective-permute-start | bytes 12296 | tf_op jit(solution)/shard_map/ppermute | solution.py:13
  19.2 293.1 %all-gather.13.cloned.1.call-start = ((), (), s32[]{:S(2)}) async-start(), calls=%async_computation.3 | async-start | bytes 4259840 | tf_op jit(solution)/shard_map/all_gather | solution.py:18
  32.1 38.2 %copy-start.3 = (bf16[128,1024]{1,0:T(8,128)(2,1)S(1)}, bf16[128,1024]{1,0:T(8,128)(2,1)}, u32[]{:S(2)}) copy-start(bf16[128,1024]{1,0:T(8,128)(2,1)} %param.12) | copy-start | bytes 786436
  37.3 41.7 %copy-start.2 = (f32[1024,16]{0,1:T(8,128)S(1)}, f32[1024,16]{0,1:T(8,128)}, u32[]{:S(2)}) copy-start(f32[1024,16]{0,1:T(8,128)} %param.17) | copy-start | bytes 196612
  69.6 0.6 copy-start
  69.6 9.4 %copy-start.1 = (f32[16,1024,16]{1,2,0:T(8,128)S(1)}, f32[16,1024,16]{1,2,0:T(8,128)}, u32[]{:S(2)}) copy-start(f32[16,1024,16]{1,2,0:T(8,128)} %get-tuple-element.132) | copy-start | bytes 3145732
  70.2 373.5 %all-gather.7.cloned.1.call-start = ((), (), s32[]{:S(2)}) async-start(), calls=%async_computation | async-start | bytes 2359296 | tf_op jit(solution)/shard_map/all_gather | solution.py:137
  70.3 23.2 %collective-permute-start = (bf16[2,1024]{1,0:T(2,128)(2,1)S(1)}, bf16[2,1024]{1,0:T(2,128)(2,1)S(1)}, u32[]{:S(2)}, u32[]{:S(2)}) collective-permute-start(bf16[2,1024]{1,0:T(2,128)(2,1)S(1)} %slice.138), channel_id=1, source_target_pairs={{0,8},{8,16},{16,24},{24,32},{32,40},{40,48},{48,56},{56,64},{64,7... | collective-permute-start | bytes 12296 | tf_op jit(solution)/shard_map/ppermute | solution.py:13
  415.8 188.4 %all-gather.9.cloned.1.call-start = ((), (), s32[]{:S(2)}) async-start(), calls=%async_computation.1 | async-start | bytes 8519680 | tf_op jit(solution)/shard_map/all_gather | solution.py:140
Sparse Core Ops, SparseCore 0:
  19.3 148.6 all-gather.10
  171.0 141.2 all-gather.12
  415.9 27.7 all-gather.6
  446.5 157.6 all-gather.8
where the time goes:
time: 619 us; the launch traced here: 617 us
  waiting for transfers between devices  401 us (65%)
  local copies, waits for them, and re-layouts  133 us (21%)
  other arithmetic  32.3 us (5%)
  matrix products  22.1 us (4%)
  between operations  14.1 us (2%)
  starting transfers between devices  12.8 us (2%)
    all_gather x2, waiting for transfers between devices, carried_in(): everything = jax.tree.map(lambda part: lax.all_gather(part, axis), x)  212 us
    all_gather x1, waiting for transfers between devices, local(): lax.all_gather(out_weight, 'ctx', axis=0, tiled=True)  160 us
    dynamic_slice x64, local copies, waits for them, and re-layouts, hop(): new = combine(before, jax.tree.map(lambda part: part[k], everything))  83.4 us
    all_gather x1, waiting for transfers between devices, local(): all_channels = lax.all_gather(gated, 'ch', axis=1, tiled=True)  27.3 us
    unnamed x11, local copies, waits for them, and re-layouts  18.9 us
    ppermute x3, starting transfers between devices, shifted(): return lax.ppermute(block, axis, route)  12.7 us
  transfers between devices with their start and end apart: 7, of which 4 were waited for; matrix products, arithmetic and copies ran while one was open for 13% of the time, Pallas kernels for 0%

commit v1 on v0

--- a/solution.py
+++ b/solution.py
@@ -5,6 +5,17 @@
 
 MODES = 16
 KS = 3
+
+
+def around_the_ring(shard, name, dim):
+    n_dev = lax.axis_size(name)
+    right = [(i, (i + 1) % n_dev) for i in range(n_dev)]
+    parts = [shard]
+    for reach in range(1, n_dev):
+        parts = [lax.ppermute(parts[0], name, right), *parts]
+    out = jnp.concatenate(parts, axis=dim)
+    shift = (lax.axis_index(name) + 1) * parts[-1].shape[dim]
+    return jnp.roll(out, shift, axis=dim)
 
 
 def shifted(block, axis, distance):
@@ -134,7 +145,7 @@
     untouched = (ages > local_index).astype(jnp.float32)[:, None]
     filtered = within + between.reshape(row_count, channels) + correction * untouched
     gated = (query_conv * filtered).astype(jnp.bfloat16)
-    all_channels = lax.all_gather(gated, "ch", axis=1, tiled=True)
+    all_channels = around_the_ring(gated, "ch", 1)
     result = jnp.dot(
         all_channels,
         lax.all_gather(out_weight, "ctx", axis=0, tiled=True),

time: 619 us -> 492 us (0.79)
  waiting for transfers between devices: 401 us -> 263 us
  local copies, waits for them, and re-layouts: 133 us -> 145 us
    all_gather x1, waiting for transfers between devices: 160 us -> 0.01 us  [local(): lax.all_gather(out_weight, 'ctx', axis=0, tiled=True)]
    ppermute x0 -> x7, waiting for transfers between devices: none -> 49 us  [around_the_ring(): parts = [lax.ppermute(parts[0], name, right), *parts]]
    all_gather x1 -> x0, waiting for transfers between devices: 27.3 us -> none  [local(): all_channels = lax.all_gather(gated, 'ch', axis=1, tiled=True)]
    unnamed x11 -> x26, local copies, waits for them, and re-layouts: 18.9 us -> 30.3 us
  transfers between devices with their start and end apart: 7 -> 13, of which waited for: 4 -> 9; matrix products, arithmetic and copies ran while one was open for 13% -> 39% of each run, Pallas kernels for 0% -> 0%
where the time goes in v1:
time: 492 us; the launch traced here: 489 us
  waiting for transfers between devices  263 us (53%)
  local copies, waits for them, and re-layouts  145 us (29%)
  other arithmetic  30.7 us (6%)
  matrix products  22.1 us (4%)
  between operations  14.1 us (3%)
  starting transfers between devices  12.8 us (3%)
    all_gather x2, waiting for transfers between devices, carried_in(): everything = jax.tree.map(lambda part: lax.all_gather(part, axis), x)  214 us
    dynamic_slice x64, local copies, waits for them, and re-layouts, hop(): new = combine(before, jax.tree.map(lambda part: part[k], everything))  83.8 us
    ppermute x7, waiting for transfers between devices, around_the_ring(): parts = [lax.ppermute(parts[0], name, right), *parts]  49 us
    unnamed x26, local copies, waits for them, and re-layouts  30.3 us
    ppermute x3, starting transfers between devices, shifted(): return lax.ppermute(block, axis, route)  12.7 us
    add x16, other arithmetic, advance(): return (block_decay * kept * state + ending, state)  10.4 us
    dynamic_update_slice x16, other arithmetic, local(): lax.scan(advance, jnp.zeros((channels, MODES), jnp.float32), (endings, un...  10 us
  transfers between devices with their start and end apart: 13, of which 9 were waited for; matrix products, arithmetic and copies ran while one was open for 39% of the time, Pallas kernels for 0%

profile of v1, /device:TPU:32, one launch (start us, length us, event | category | flops | bytes accessed | tf_op | source)
XLA Modules:
  0.0 489.3 jit_solution(255535532311788185)
XLA Ops:
  7.3 3.8 collective-permute-start.1
  11.8 3.8 collective-permute-start.2
  17.6 1.6 fusion.65
  23.6 2.8 copy.59
  26.3 5.7 %fusion.16 = f32[16,1024,16]{2,0,1:T(8,128)} fusion(f32[16,8,1024]{0,1,2:T(8,128)} %copy.59, f32[1024,16]{1,0:T(8,128)S(1)} %copy.60, f32[8]{0:T(128)S(1)} %iota_subtract_fusion, f32[16,8]{0,1:T(8,128)S(1)} %compare_convert_fusion, f32[1024,16]{1,0:T(8,128)S(1)} %copy.57), kind=kOutput, calls=%fused_computation.25 | convolution fusion | flops 4587520 | bytes 1704480 | tf_op jit(solution)/shard_map/rcm,brc->bcm/dot_general | solution.py:121
  32.1 5.2 %copy.61 = f32[16,1024,16]{1,2,0:T(8,128)S(1)} copy(f32[16,1024,16]{2,0,1:T(8,128)} %fusion.16) | data formatting | bytes 2097152
  37.3 30.5 %while.27 = (s32[]{:T(128)}, f32[1024,16]{0,1:T(8,128)S(1)}, f32[16,1024,16]{1,2,0:T(8,128)}, f32[16]{0:T(128)S(1)}, f32[1024,16]{0,1:T(8,128)S(1)}, /*index=5*/f32[16,1024,16]{1,2,0:T(8,128)S(1)}, s32[]{:T(128)}, s32[]{:T(128)}) while((s32[]{:T(128)}, f32[1024,16]{0,1:T(8,128)S(1)}, f32[16,1024,16]{1,2,0:T(8,128)}, ...), condition=%wide.region_3.4_spmd.clone, body=%wide.region_2.3_spmd.clone.sunk | while | flops 81923 | bytes 393844 | solution.py:128
  68.5 5.0 %collective-permute-start = (bf16[2,1024]{1,0:T(2,128)(2,1)S(1)}, bf16[2,1024]{1,0:T(2,128)(2,1)S(1)}, u32[]{:S(2)}, u32[]{:S(2)}) collective-permute-start(bf16[2,1024]{1,0:T(2,128)(2,1)S(1)} %slice.138), channel_id=1, source_target_pairs={{0,8},{8,16},{16,24},{24,32},{32,40},{40,48},{48,56},{56,64},{64,7... | collective-permute-start | bytes 12296 | tf_op jit(solution)/shard_map/ppermute | solution.py:24
  75.1 2.1 slice_reduce_fusion.7
  77.4 4.9 %copy.62 = bf16[16,1024,16]{2,0,1:T(8,128)(2,1)} copy(bf16[16,1024,16]{1,2,0:T(8,128)(2,1)S(1)} %broadcast_multiply_fusion) | data formatting | bytes 1048576 | tf_op jit(solution)/shard_map/mul | solution.py:133
  82.3 6.5 %multiply_bitcast_fusion = f32[16,8,1024]{0,1,2:T(8,128)} fusion(bf16[16,1024,16]{2,0,1:T(8,128)(2,1)} %copy.62, f32[16,8]{0,1:T(8,128)S(1)} %copy.63, f32[8]{0:T(128)S(1)} %iota_add_fusion, f32[1024,16]{1,0:T(8,128)S(1)} %copy.57), kind=kOutput, calls=%fused_computation.16 | convolution fusion | flops 4456448 | bytes 1114656 | tf_op jit(solution)/shard_map/rcm,bcm->brc/dot_general | solution.py:133
  88.8 3.0 copy.64
  91.9 76.0 %all-gather.8.cloned.1.call-done = f32[65536,16]{0,1:T(8,128)} async-done(((f32[1024,16]{0,1:T(8,128)}), f32[65536,16]{0,1:T(8,128)}) %all-gather.8.cloned.1.call-update) | async-done | bytes 4194320 | tf_op jit(solution)/shard_map/all_gather | solution.py:29
  167.9 6.6 %copy.72 = f32[2,8,64,1024]{3,2,1,0:T(8,128)} copy(f32[2,8,64,1024]{3,1,2,0:T(8,128)} %bitcast.67) | data formatting | bytes 8388608
  174.5 137.7 %all-gather.10.cloned.1.call-done = f32[65536,16]{0,1:T(8,128)} async-done(((f32[1024,16]{0,1:T(8,128)}), f32[65536,16]{0,1:T(8,128)}) %all-gather.10.cloned.1.call-update) | async-done | bytes 4194320 | tf_op jit(solution)/shard_map/all_gather | solution.py:29
  312.2 6.6 %copy.73 = f32[2,8,64,1024]{3,2,1,0:T(8,128)} copy(f32[2,8,64,1024]{3,1,2,0:T(8,128)} %bitcast.68) | data formatting | bytes 8388608
  318.8 88.4 %while.28 = (s32[]{:T(128)}, f32[1024,16]{0,1:T(8,128)S(1)}, s32[]{:T(128)}, f32[64,1024,16]{1,0,2:T(8,128)}, f32[64,1024,16]{1,0,2:T(8,128)}, /*index=5*/s32[]{:T(128)}, s32[]{:T(128)}) while((s32[]{:T(128)}, f32[1024,16]{0,1:T(8,128)S(1)}, s32[]{:T(128)}, f32[64,1024,16]{1,0,2:T(8,128)}, f32[64,1024,16]{1,0,2:T(8,128)}, ...), condition=%wide.region_5.6_spmd.clone, body=%wide.region_4.5_spmd.clone.sunk | while | flops 65540 | bytes 524389 | solution.py:39
  331.2 1.3 constant_dynamic-slice_fusion.3
  335.3 1.3 constant_dynamic-slice_fusion.3
  339.5 1.3 constant_dynamic-slice_fusion.3
  343.6 1.3 constant_dynamic-slice_fusion.3
  346.4 1.3 constant_dynamic-slice_fusion.3
  349.1 1.3 constant_dynamic-slice_fusion.3
  350.5 1.3 constant_dynamic-slice_fusion.3
  354.6 1.3 constant_dynamic-slice_fusion.3
  357.4 1.3 constant_dynamic-slice_fusion.3
  358.8 1.3 constant_dynamic-slice_fusion.3
  361.5 1.3 constant_dynamic-slice_fusion.3
  365.7 1.3 constant_dynamic-slice_fusion.3
  369.8 1.3 constant_dynamic-slice_fusion.3
  371.2 1.3 constant_dynamic-slice_fusion.3
  373.9 1.3 constant_dynamic-slice_fusion.3
  375.3 1.3 constant_dynamic-slice_fusion.3
  379.4 1.3 constant_dynamic-slice_fusion.3
  395.9 1.5 constant_dynamic-slice_fusion.3
  403.0 1.3 constant_dynamic-slice_fusion.3
  404.4 1.3 constant_dynamic-slice_fusion.3
  405.8 1.3 constant_dynamic-slice_fusion.3
  407.4 3.9 fusion.21
  411.3 3.3 copy.69
  415.7 7.0 %collective-permute-done.3 = bf16[128,1024]{1,0:T(8,128)(2,1)S(1)} collective-permute-done((bf16[128,1024]{1,0:T(8,128)(2,1)S(1)}, bf16[128,1024]{1,0:T(8,128)(2,1)S(1)}, u32[]{:S(2)}, u32[]{:S(2)}) %collective-permute-start.3) | collective-permute-done | bytes 262176 | tf_op jit(solution)/shard_map/ppermute | solution.py:15
  422.7 7.0 %collective-permute-done.4 = bf16[128,1024]{1,0:T(8,128)(2,1)S(1)} collective-permute-done((bf16[128,1024]{1,0:T(8,128)(2,1)S(1)}, bf16[128,1024]{1,0:T(8,128)(2,1)S(1)}, u32[]{:S(2)}, u32[]{:S(2)}) %collective-permute-start.4) | collective-permute-done | bytes 262176 | tf_op jit(solution)/shard_map/ppermute | solution.py:15
  429.7 7.0 %collective-permute-done.5 = bf16[128,1024]{1,0:T(8,128)(2,1)S(1)} collective-permute-done((bf16[128,1024]{1,0:T(8,128)(2,1)S(1)}, bf16[128,1024]{1,0:T(8,128)(2,1)S(1)}, u32[]{:S(2)}, u32[]{:S(2)}) %collective-permute-start.5) | collective-permute-done | bytes 262176 | tf_op jit(solution)/shard_map/ppermute | solution.py:15
  436.7 7.0 %collective-permute-done.6 = bf16[128,1024]{1,0:T(8,128)(2,1)S(1)} collective-permute-done((bf16[128,1024]{1,0:T(8,128)(2,1)S(1)}, bf16[128,1024]{1,0:T(8,128)(2,1)S(1)}, u32[]{:S(2)}, u32[]{:S(2)}) %collective-permute-start.6) | collective-permute-done | bytes 262176 | tf_op jit(solution)/shard_map/ppermute | solution.py:15
  443.7 7.0 %collective-permute-done.7 = bf16[128,1024]{1,0:T(8,128)(2,1)S(1)} collective-permute-done((bf16[128,1024]{1,0:T(8,128)(2,1)S(1)}, bf16[128,1024]{1,0:T(8,128)(2,1)S(1)}, u32[]{:S(2)}, u32[]{:S(2)}) %collective-permute-start.7) | collective-permute-done | bytes 262176 | tf_op jit(solution)/shard_map/ppermute | solution.py:15
  450.7 7.0 %collective-permute-done.8 = bf16[128,1024]{1,0:T(8,128)(2,1)S(1)} collective-permute-done((bf16[128,1024]{1,0:T(8,128)(2,1)S(1)}, bf16[128,1024]{1,0:T(8,128)(2,1)S(1)}, u32[]{:S(2)}, u32[]{:S(2)}) %collective-permute-start.8) | collective-permute-done | bytes 262176 | tf_op jit(solution)/shard_map/ppermute | solution.py:15
  457.7 7.0 %collective-permute-done.9 = bf16[128,1024]{1,0:T(8,128)(2,1)S(1)} collective-permute-done((bf16[128,1024]{1,0:T(8,128)(2,1)S(1)}, bf16[128,1024]{1,0:T(8,128)(2,1)S(1)}, u32[]{:S(2)}, u32[]{:S(2)}) %collective-permute-start.9) | collective-permute-done | bytes 262176 | tf_op jit(solution)/shard_map/ppermute | solution.py:15
  476.8 5.9 %fusion.34 = bf16[128,512]{1,0:T(8,128)(2,1)} fusion(bf16[8192,512]{1,0:T(8,128)(2,1)} %all-gather.6.cloned.1.call-done, bf16[128,16384]{1,0:T(8,128)(2,1)} %constant_dynamic-update-slice_fusion, s32[]{:T(128)S(6)} %select_n.73), kind=kOutput, calls=%fused_computation.37 | convolution fusion | flops 1073807360 | bytes 10616836 | tf_op jit(solution)/shard_map/dot_general | solution.py:149
  (230 shorter events, 111.8 us)
Async XLA Ops:
  6.5 161.4 %all-gather.8.cloned.1.call-start = ((), (), s32[]{:S(2)}) async-start(), calls=%async_computation.1 | async-start | bytes 4259840 | tf_op jit(solution)/shard_map/all_gather | solution.py:29
  7.3 13.7 %collective-permute-start.1 = (bf16[2,1024]{1,0:T(2,128)(2,1)S(1)}, bf16[2,1024]{1,0:T(2,128)(2,1)S(1)}, u32[]{:S(2)}, u32[]{:S(2)}) collective-permute-start(bf16[2,1024]{1,0:T(2,128)(2,1)S(1)} %slice.146), channel_id=1, source_target_pairs={{0,8},{8,16},{16,24},{24,32},{32,40},{40,48},{48,56},{56,64},{64,7... | collective-permute-start | bytes 12296 | tf_op jit(solution)/shard_map/ppermute | solution.py:24
  11.8 10.2 %collective-permute-start.2 = (bf16[2,1024]{1,0:T(2,128)(2,1)S(1)}, bf16[2,1024]{1,0:T(2,128)(2,1)S(1)}, u32[]{:S(2)}, u32[]{:S(2)}) collective-permute-start(bf16[2,1024]{1,0:T(2,128)(2,1)S(1)} %slice.153), channel_id=1, source_target_pairs={{0,8},{8,16},{16,24},{24,32},{32,40},{40,48},{48,56},{56,64},{64,7... | collective-permute-start | bytes 12296 | tf_op jit(solution)/shard_map/ppermute | solution.py:24
  19.2 293.0 %all-gather.10.cloned.1.call-start = ((), (), s32[]{:S(2)}) async-start(), calls=%async_computation.2 | async-start | bytes 4259840 | tf_op jit(solution)/shard_map/all_gather | solution.py:29
  32.1 36.4 %copy-start.3 = (bf16[128,1024]{1,0:T(8,128)(2,1)S(1)}, bf16[128,1024]{1,0:T(8,128)(2,1)}, u32[]{:S(2)}) copy-start(bf16[128,1024]{1,0:T(8,128)(2,1)} %param.12) | copy-start | bytes 786436
  37.3 40.0 %copy-start.2 = (f32[1024,16]{0,1:T(8,128)S(1)}, f32[1024,16]{0,1:T(8,128)}, u32[]{:S(2)}) copy-start(f32[1024,16]{0,1:T(8,128)} %param.17) | copy-start | bytes 196612
  67.8 0.6 copy-start
  67.8 9.5 %copy-start.1 = (f32[16,1024,16]{1,2,0:T(8,128)S(1)}, f32[16,1024,16]{1,2,0:T(8,128)}, u32[]{:S(2)}) copy-start(f32[16,1024,16]{1,2,0:T(8,128)} %get-tuple-element.132) | copy-start | bytes 3145732
  68.5 408.3 %all-gather.6.cloned.1.call-start = ((), (), s32[]{:S(2)}) async-start(), calls=%async_computation | async-start | bytes 8519680 | tf_op jit(solution)/shard_map/all_gather | solution.py:151
  68.5 23.3 %collective-permute-start = (bf16[2,1024]{1,0:T(2,128)(2,1)S(1)}, bf16[2,1024]{1,0:T(2,128)(2,1)S(1)}, u32[]{:S(2)}, u32[]{:S(2)}) collective-permute-start(bf16[2,1024]{1,0:T(2,128)(2,1)S(1)} %slice.138), channel_id=1, source_target_pairs={{0,8},{8,16},{16,24},{24,32},{32,40},{40,48},{48,56},{56,64},{64,7... | collective-permute-start | bytes 12296 | tf_op jit(solution)/shard_map/ppermute | solution.py:24
  415.7 7.0 %collective-permute-start.3 = (bf16[128,1024]{1,0:T(8,128)(2,1)S(1)}, bf16[128,1024]{1,0:T(8,128)(2,1)S(1)}, u32[]{:S(2)}, u32[]{:S(2)}) collective-permute-start(bf16[128,1024]{1,0:T(8,128)(2,1)S(1)} %fusion.52), channel_id=1, source_target_pairs={{0,1},{1,2},{2,3},{3,4},{4,5},{5,6},{6,7},{7,0},{8,9},{9,10},{10,1... | collective-permute-start | bytes 786440 | tf_op jit(solution)/shard_map/ppermute | solution.py:15
  422.7 7.0 %collective-permute-start.4 = (bf16[128,1024]{1,0:T(8,128)(2,1)S(1)}, bf16[128,1024]{1,0:T(8,128)(2,1)S(1)}, u32[]{:S(2)}, u32[]{:S(2)}) collective-permute-start(bf16[128,1024]{1,0:T(8,128)(2,1)S(1)} %collective-permute-done.3), channel_id=1, source_target_pairs={{0,1},{1,2},{2,3},{3,4},{4,5},{5,6},{6,7},{7,0},{8,9},{9,10},{10,1... | collective-permute-start | bytes 786440 | tf_op jit(solution)/shard_map/ppermute | solution.py:15
  429.7 7.0 %collective-permute-start.5 = (bf16[128,1024]{1,0:T(8,128)(2,1)S(1)}, bf16[128,1024]{1,0:T(8,128)(2,1)S(1)}, u32[]{:S(2)}, u32[]{:S(2)}) collective-permute-start(bf16[128,1024]{1,0:T(8,128)(2,1)S(1)} %collective-permute-done.4), channel_id=1, source_target_pairs={{0,1},{1,2},{2,3},{3,4},{4,5},{5,6},{6,7},{7,0},{8,9},{9,10},{10,1... | collective-permute-start | bytes 786440 | tf_op jit(solution)/shard_map/ppermute | solution.py:15
  436.7 7.0 %collective-permute-start.6 = (bf16[128,1024]{1,0:T(8,128)(2,1)S(1)}, bf16[128,1024]{1,0:T(8,128)(2,1)S(1)}, u32[]{:S(2)}, u32[]{:S(2)}) collective-permute-start(bf16[128,1024]{1,0:T(8,128)(2,1)S(1)} %collective-permute-done.5), channel_id=1, source_target_pairs={{0,1},{1,2},{2,3},{3,4},{4,5},{5,6},{6,7},{7,0},{8,9},{9,10},{10,1... | collective-permute-start | bytes 786440 | tf_op jit(solution)/shard_map/ppermute | solution.py:15
  443.7 7.0 %collective-permute-start.7 = (bf16[128,1024]{1,0:T(8,128)(2,1)S(1)}, bf16[128,1024]{1,0:T(8,128)(2,1)S(1)}, u32[]{:S(2)}, u32[]{:S(2)}) collective-permute-start(bf16[128,1024]{1,0:T(8,128)(2,1)S(1)} %collective-permute-done.6), channel_id=1, source_target_pairs={{0,1},{1,2},{2,3},{3,4},{4,5},{5,6},{6,7},{7,0},{8,9},{9,10},{10,1... | collective-permute-start | bytes 786440 | tf_op jit(solution)/shard_map/ppermute | solution.py:15
  450.7 7.0 %collective-permute-start.8 = (bf16[128,1024]{1,0:T(8,128)(2,1)S(1)}, bf16[128,1024]{1,0:T(8,128)(2,1)S(1)}, u32[]{:S(2)}, u32[]{:S(2)}) collective-permute-start(bf16[128,1024]{1,0:T(8,128)(2,1)S(1)} %collective-permute-done.7), channel_id=1, source_target_pairs={{0,1},{1,2},{2,3},{3,4},{4,5},{5,6},{6,7},{7,0},{8,9},{9,10},{10,1... | collective-permute-start | bytes 786440 | tf_op jit(solution)/shard_map/ppermute | solution.py:15
  457.7 7.0 %collective-permute-start.9 = (bf16[128,1024]{1,0:T(8,128)(2,1)S(1)}, bf16[128,1024]{1,0:T(8,128)(2,1)S(1)}, u32[]{:S(2)}, u32[]{:S(2)}) collective-permute-start(bf16[128,1024]{1,0:T(8,128)(2,1)S(1)} %collective-permute-done.8), channel_id=1, source_target_pairs={{0,1},{1,2},{2,3},{3,4},{4,5},{5,6},{6,7},{7,0},{8,9},{9,10},{10,1... | collective-permute-start | bytes 786440 | tf_op jit(solution)/shard_map/ppermute | solution.py:15
Sparse Core Ops, SparseCore 0:
  19.3 148.5 all-gather.7
  170.9 141.2 all-gather.9
  315.1 152.1 all-gather.5
